TPU v7x, 32 devices: a whole 2x2x4 slice. The times are simulated.
32 devices in a mesh: ctx: 4 (over y, core), ch: 8 (over z, x).
Axes of the slice: x: 2, y: 2, z: 4, core: 2. Of those that a mesh axis runs over, the one named last changes fastest.
Arguments:
- tokens: bfloat16 [4096, 4096], P('ctx', 'ch'), may hold values from -6 to 6
- in_weight: bfloat16 [3, 4096, 4096], P(None, None, 'ch'), may hold values from -0.09375 to 0.09375
- short_filters: float32 [3, 3, 4096], P(None, None, 'ch'), may hold values from -3 to 3
- log_rates: float32 [16, 4096], P(None, 'ch'), may hold values from 0.1 to 500
- residues: float32 [16, 4096], P(None, 'ch'), may hold values from -0.06 to 0.06
- skip_gain: float32 [4096], P('ch'), may hold values from -4 to 4
- out_weight: bfloat16 [4096, 4096], P('ch'), may hold values from -0.125 to 0.125
Outputs:
- block_out: bfloat16 [4096, 4096], P('ctx', 'ch')
All inputs are finite; a program needn't handle non-finite values.
Results may differ from a plain program's by a relative error of at most 0.008.
Values may be sent and summed in bfloat16 or wider, within the bound.
A program may use at most 192 MiB of HBM per device.

v0:
```python
import jax
import jax.numpy as jnp
from jax import lax
from jax.sharding import PartitionSpec as P

HIGH = lax.Precision.HIGHEST


def from_behind(value, axis, steps):
    count = lax.axis_size(axis)
    leading, last = (max(0, -steps), min(count, count - steps))
    return lax.ppermute(value, axis, [(source, source + steps) for source in range(leading, last)])


def prefix(array, axis, join, neutral):
    place = lax.axis_index(axis)
    gathered = jax.tree.map(
        lambda a, kind: lax.all_gather(a.astype(kind), axis), array, (jnp.bfloat16, jnp.bfloat16)
    )
    state = jax.tree.map(lambda a, e: jnp.zeros_like(a) + jnp.asarray(e, a.dtype), array, neutral)

    def one(hop, state):
        return join(
            state,
            jax.tree.map(
                lambda a, own: lax.dynamic_index_in_dim(a, hop, 0, False).astype(own.dtype),
                gathered,
                array,
            ),
        )

    return lax.fori_loop(0, place, one, state)


def join_states(earlier, later):
    return (earlier[0] * later[0], later[0] * earlier[1] + later[1])


def shards(tokens, in_weight, short_filters, log_rates, residues, skip_gain, out_weight):
    rows = tokens.shape[0]
    cols = in_weight.shape[2]
    seq = rows * lax.axis_size("ctx")
    taps = short_filters.shape[1]
    projected = jnp.einsum(
        "tk,pkc->ptc",
        lax.all_gather(tokens, "ch", axis=1, tiled=True),
        in_weight,
        preferred_element_type=jnp.float32,
    ).astype(jnp.bfloat16)
    previous = from_behind(projected[:, rows - (taps - 1) :, :], "ctx", 1)
    extended = jnp.concatenate([previous, projected], axis=1).astype(jnp.float32)
    featured = jnp.zeros((3, rows, cols), jnp.float32)
    for lag in range(taps):
        featured = (
            featured
            + short_filters[:, lag, None, :]
            * extended[:, taps - 1 - lag : taps - 1 - lag + rows, :]
        )
    query, keyed, valued = (featured[0], featured[1], featured[2])
    mixed_in = keyed * valued
    block = min(128, rows)
    count = rows // block
    rate = log_rates / seq
    offsets = jnp.arange(block, dtype=jnp.float32)
    powers = jnp.exp(-offsets[:, None, None] * rate[None])
    kernel_rows = jnp.einsum("dmc,mc->dc", powers, residues, precision=HIGH)
    lag_grid = jnp.arange(block)[:, None] - jnp.arange(block)[None, :]
    toeplitz = jnp.where(
        lag_grid[:, :, None] >= 0, jnp.take(kernel_rows, jnp.maximum(lag_grid, 0), axis=0), 0.0
    )
    blocks = mixed_in.reshape(count, block, cols)
    inner = jnp.einsum("ijc,njc->nic", toeplitz, blocks, precision=HIGH)
    ends = jnp.einsum("jmc,njc->nmc", powers[::-1], blocks, precision=HIGH)
    positions = jnp.arange(count)
    tail_weights = jnp.exp(
        -rate[None] * (block * (count - 1 - positions)).astype(jnp.float32)[:, None, None]
    )
    local_state = jnp.sum(tail_weights * ends, axis=0)
    device_decay = jnp.exp(-rate * rows)
    identity = (jnp.ones_like(device_decay), jnp.zeros_like(local_state))
    incoming = prefix((device_decay, local_state), "ctx", join_states, identity)[1]
    gaps = positions[:, None] - 1 - positions[None, :]
    coupling = jnp.where(
        (gaps >= 0)[:, :, None, None],
        jnp.exp(
            -rate[None, None] * block * jnp.maximum(gaps, 0).astype(jnp.float32)[:, :, None, None]
        ),
        0.0,
    )
    lead_in = jnp.exp(-rate[None] * (block * positions).astype(jnp.float32)[:, None, None])
    starts = jnp.einsum("npmc,pmc->nmc", coupling, ends, precision=HIGH) + lead_in * incoming[None]
    reach = jnp.exp(-(offsets[:, None, None] + 1.0) * rate[None]) * residues[None]
    crossed = jnp.einsum("imc,nmc->nic", reach, starts, precision=HIGH)
    convolved = (inner + crossed).reshape(rows, cols) + skip_gain[None, :] * mixed_in
    gated = (query * convolved).astype(jnp.bfloat16)
    column_weight = lax.all_to_all(out_weight, "ch", split_axis=1, concat_axis=0, tiled=True)
    summed = jnp.dot(
        lax.all_gather(gated, "ch", axis=1, tiled=True),
        column_weight,
        preferred_element_type=jnp.float32,
    )
    return summed.astype(jnp.bfloat16)


def solution(mesh):
    return jax.shard_map(
        shards,
        mesh=mesh,
        in_specs=(
            P("ctx", "ch"),
            P(None, None, "ch"),
            P(None, None, "ch"),
            P(None, "ch"),
            P(None, "ch"),
            P("ch"),
            P("ch", None),
        ),
        out_specs=P("ctx", "ch"),
        check_vma=False,
    )
```

profile of v0, /device:TPU:0, one launch (start us, length us, event | category | flops | bytes accessed | tf_op | source)
XLA Modules:
  0.0 595.2 jit_solution(11589461095154466215)
XLA Ops:
  15.4 6.7 %multiply_reduce_fusion = f32[512,128]{1,0:T(8,128)} fusion(f32[512,16]{1,0:T(8,128)S(1)} %copy.82, f32[16,512]{0,1:T(8,128)S(1)} %copy.56, f32[128]{0:T(128)S(1)} %iota_negate_fusion), kind=kLoop, calls=%fused_computation.17 | loop fusion | flops 3080192 | bytes 328192
  22.1 3.6 multiply_exponential_fusion
  25.7 111.8 %all-gather.5.cloned.1.call-done = bf16[1024,4096]{1,0:T(8,128)(2,1)} async-done(((bf16[1024,512]{1,0:T(8,128)(2,1)}), bf16[1024,4096]{1,0:T(8,128)(2,1)}) %all-gather.5.cloned.1.call-update) | async-done | bytes 8388624 | tf_op jit(solution)/shard_map/all_gather | solution.py:46
  137.5 18.3 %convert_bitcast_fusion = bf16[3,1024,512]{1,2,0:T(8,128)(2,1)S(1)} fusion(bf16[3,4096,512]{2,1,0:T(8,128)(2,1)} %param.10, bf16[1024,4096]{1,0:T(8,128)(2,1)} %all-gather.5.cloned.1.call-done), kind=kOutput, calls=%fused_computation.24 | convolution fusion | flops 12886474752 | bytes 24117248 | tf_op jit(solution)/shard_map/tk,pkc->ptc/dot_general | solution.py:44
  156.8 2.0 collective-permute-start
  158.8 5.9 all-gather
  164.8 1.6 copy.61
  167.1 7.2 %rev.3 = f32[128,16,512]{0,1,2:T(8,128)} reverse(f32[128,16,512]{0,1,2:T(8,128)} %multiply_exponential_fusion), dimensions={0} | reverse | bytes 8388608 | tf_op jit(solution)/shard_map/rev | solution.py:73
  176.2 64.1 %gather_fusion = f32[16384,512]{1,0:T(8,128)} fusion(f32[128,512]{1,0:T(8,128)S(1)} %bitcast.78, s32[16384]{0:T(1024)S(1)} %bitcast_clamp_fusion), kind=kCustom, calls=%fused_computation | custom fusion | bytes 67174400 | tf_op jit(solution)/shard_map/jit(_take)/gather | solution.py:69
  240.3 35.6 %copy.57 = f32[128,128,512]{1,0,2:T(8,128)} copy(f32[128,128,512]{2,1,0:T(8,128)} %bitcast.79) | data formatting | bytes 67108864 | tf_op jit(solution)/shard_map/jit(_take)/gather | solution.py:69
  275.9 2.7 maximum_convert_fusion
  278.6 5.2 fusion.9
  284.9 2.1 copy-done
  288.4 8.1 %fusion.19 = (bf16[16,512]{0,1:T(8,128)(2,1)S(1)}, f32[512,8,16]{2,1,0:T(8,128)}) fusion(f32[8]{0:T(128)S(1)} %copy-done.13, f32[16,512]{0,1:T(8,128)S(1)} %copy-done.4, f32[8,128,512]{1,0,2:T(8,128)S(1)} %bitcast.82, f32[128,16,512]{0,1,2:T(8,128)S(1)} %copy-done.1), kind=kOutput, calls=%fused_computation.33 | convolution fusion | flops 100851712 | bytes 6602784 | tf_op jit(solution)/shard_map/jmc,njc->nmc/dot_general | solution.py:73
  296.5 2.2 copy.83
  299.2 2.0 copy.78
  301.3 7.3 %all-gather.1 = bf16[64,512]{1,0:T(8,128)(2,1)S(1)} all-gather(bf16[16,512]{1,0:T(8,128)(2,1)S(1)} %copy.59), channel_id=3, replica_groups=mesh['ctx'=4,'ch'=8] {'ctx'}, dimensions={0}, use_global_device_ids=true | all-gather | bytes 81920 | tf_op jit(solution)/shard_map/all_gather | solution.py:18
  308.8 8.3 %fusion.11 = f32[512,8,128]{2,1,0:T(8,128)S(1)} fusion(f32[16,512,8]{0,2,1:T(8,128)} %copy.78, f32[16,512]{0,1:T(8,128)} %copy.61, f32[128]{0:T(128)S(1)} %copy-done.15, f32[16,512]{0,1:T(8,128)S(1)} %copy-done.3, f32[16,512]{0,1:T(8,128)S(1)} %copy.60, f32[8]{0:T(128)S(1)} %copy-done.16, f32[16,512]{0,1:T(8,128)S(1)} %copy-done.4), kind=kOutput, calls=%fused_computation.18 | convolution fusion | flops 102957056 | bytes 2490912 | tf_op jit(solution)/shard_map/imc,nmc->nic/dot_general | solution.py:93
  317.1 56.0 %fusion.26 = f32[512,8,128]{2,1,0:T(8,128)S(1)} fusion(f32[512,8,128]{2,1,0:T(8,128)S(1)} %fusion.11, f32[8,128,512]{1,0,2:T(8,128)S(1)} %bitcast.83, f32[128,128,512]{1,0,2:T(8,128)} %copy.57, pred[128,128]{1,0:T(8,128)(4,1)S(1)} %copy-done.5, pred[128,128]{1,0:T(8,128)(4,1)S(1)} %copy-done.6), kind=kOutput, calls=%fused_computation.41 | convolution fusion | flops 822607872 | bytes 39878656 | tf_op jit(solution)/shard_map/ijc,njc->nic/dot_general | solution.py:72
  374.7 6.4 %copy.62 = bf16[512,4096]{0,1:T(8,128)(2,1)} copy(bf16[512,4096]{1,0:T(8,128)(2,1)} %param.15) | data formatting | bytes 8388608 | tf_op args[6]
  381.2 188.8 %all_to_all.19 = bf16[512,8,512]{0,2,1:T(8,128)(2,1)} all-to-all(bf16[512,8,512]{0,2,1:T(8,128)(2,1)} %bitcast.85), channel_id=1, replica_groups=mesh['ctx'=4,'ch'=8] {'ch'}, dimensions={1} | all-to-all | bytes 8388608 | tf_op jit(solution)/shard_map/all_to_all | solution.py:96
  570.0 6.5 %copy.63 = bf16[8,512,512]{2,1,0:T(8,128)(2,1)} copy(bf16[8,512,512]{1,2,0:T(8,128)(2,1)} %bitcast.84) | data formatting | bytes 8388608 | tf_op jit(solution)/shard_map/all_to_all | solution.py:96
  576.4 1.7 all-gather.7.cloned.1.call-done
  578.1 10.1 %convolution_convert_fusion = bf16[1024,512]{1,0:T(8,128)(2,1)} fusion(bf16[1024,4096]{0,1:T(8,128)(2,1)} %all-gather.7.cloned.1.call-done, bf16[4096,512]{1,0:T(8,128)(2,1)} %bitcast.88), kind=kOutput, calls=%fused_computation.42 | convolution fusion | flops 4295491584 | bytes 13631488 | tf_op jit(solution)/shard_map/dot_general | solution.py:97
  (69 shorter events, 17.1 us)
Async XLA Ops:
  6.5 131.0 %all-gather.5.cloned.1.call-start = ((), (), s32[]{:S(2)}) async-start(), calls=%async_computation.1 | async-start | bytes 9437184 | tf_op jit(solution)/shard_map/all_gather | solution.py:46
  7.3 570.8 %all-gather.7.cloned.1.call-start = ((), (), s32[]{:S(2)}) async-start(), calls=%async_computation.2 | async-start | bytes 9437184 | tf_op jit(solution)/shard_map/all_gather | solution.py:98
  8.8 147.1 %copy-start.2 = (f32[16,512]{0,1:T(8,128)}, f32[16,512]{0,1:T(8,128)S(1)}, u32[]{:S(2)}) copy-start(f32[16,512]{0,1:T(8,128)S(1)} %copy.56) | copy-start | bytes 98308
  156.8 119.1 %collective-permute-start = (bf16[3,2,512]{1,2,0:T(8,128)(2,1)}, bf16[3,2,512]{1,2,0:T(8,128)(2,1)}, u32[]{:S(2)}, u32[]{:S(2)}) collective-permute-start(bf16[3,2,512]{1,2,0:T(8,128)(2,1)} %slice.42), channel_id=1, source_target_pairs={{0,8},{8,16},{16,24},{1,9},{9,17},{17,25},{2,10},{10,18},{18,26},{... | collective-permute-start | bytes 18440 | tf_op jit(solution)/shard_map/ppermute | solution.py:12
  167.1 7.2 %copy-start.7 = (f32[16,512]{1,0:T(8,128)S(1)}, f32[16,512]{1,0:T(8,128)}, u32[]{:S(2)}) copy-start(f32[16,512]{1,0:T(8,128)} %get-tuple-element.65) | copy-start | bytes 98308
  275.9 2.7 copy-start.8
  275.9 2.7 copy-start.9
  283.9 3.2 copy-start
  283.9 4.5 copy-start.1
  283.9 4.5 copy-start.4
  283.9 4.5 copy-start.13
  288.4 10.3 %copy-start.10 = (f32[16,512]{1,0:T(8,128)S(1)}, f32[16,512]{1,0:T(8,128)}, u32[]{:S(2)}) copy-start(f32[16,512]{1,0:T(8,128)} %get-tuple-element.66) | copy-start | bytes 98308
  288.4 10.3 %copy-start.11 = (f32[8,8]{1,0:T(8,128)S(1)}, f32[8,8]{1,0:T(8,128)}, u32[]{:S(2)}) copy-start(f32[8,8]{1,0:T(8,128)} %maximum_convert_fusion.1) | copy-start | bytes 772
  288.4 10.3 %copy-start.14 = (pred[8,8]{1,0:T(8,128)(4,1)S(1)}, pred[8,8]{1,0:T(8,128)(4,1)}, u32[]{:S(2)}) copy-start(pred[8,8]{1,0:T(8,128)(4,1)} %fusion.34) | copy-start | bytes 196
  296.4 12.3 %copy-start.3 = (f32[16,512]{0,1:T(8,128)S(1)}, f32[16,512]{0,1:T(8,128)}, u32[]{:S(2)}) copy-start(f32[16,512]{0,1:T(8,128)} %copy-done.2) | copy-start | bytes 98308
  296.4 12.3 %copy-start.15 = (f32[128]{0:T(128)S(1)}, f32[128]{0:T(128)}, u32[]{:S(2)}) copy-start(f32[128]{0:T(128)} %add_negate_fusion) | copy-start | bytes 1540
  296.4 12.3 %copy-start.16 = (f32[8]{0:T(128)S(1)}, f32[8]{0:T(128)}, u32[]{:S(2)}) copy-start(f32[8]{0:T(128)} %multiply_convert_fusion.1) | copy-start | bytes 100
  308.6 8.5 %copy-start.5 = (pred[128,128]{1,0:T(8,128)(4,1)S(1)}, pred[128,128]{1,0:T(8,128)(4,1)}, u32[]{:S(2)}) copy-start(pred[128,128]{1,0:T(8,128)(4,1)} %get-tuple-element.76) | copy-start | bytes 49156
  308.6 8.5 %copy-start.6 = (pred[128,128]{1,0:T(8,128)(4,1)S(1)}, pred[128,128]{1,0:T(8,128)(4,1)}, u32[]{:S(2)}) copy-start(pred[128,128]{1,0:T(8,128)(4,1)} %get-tuple-element.77) | copy-start | bytes 49156
  308.8 64.3 %slice-start = ((s8[6291456]{0:T(1024)(128)(4,1)}), s8[4194304]{0:T(1024)(128)(4,1)S(1)}, s32[]{:S(2)}) async-start(s8[6291456]{0:T(1024)(128)(4,1)} %bitcast.80), calls=%async_computation.3 | async-start | bytes 8388608
  317.1 56.0 %slice-start.1 = ((s8[6291456]{0:T(1024)(128)(4,1)}), s8[2097152]{0:T(1024)(128)(4,1)S(1)}, s32[]{:S(2)}) async-start(s8[6291456]{0:T(1024)(128)(4,1)} %bitcast.80), calls=%async_computation.4 | async-start | bytes 4194304
  317.1 56.0 %copy-start.12 = (f32[512]{0:T(512)S(1)}, f32[512]{0:T(512)}, u32[]{:S(2)}) copy-start(f32[512]{0:T(512)} %param.14) | copy-start | bytes 6148
Sparse Core Ops, SparseCore 0:
  9.4 128.0 all-gather.4
  374.8 203.1 all-gather.6
where the time goes:
time: 603 us; the launch traced here: 595 us
  blocking collectives  202 us (33%)
  local copies, waits for them, and re-layouts  136 us (23%)
  waiting for transfers between devices  114 us (19%)
  matrix products  101 us (17%)
  other arithmetic  25.8 us (4%)
  between operations  14 us (2%)
    all_to_all x1, blocking collectives, shards(): lax.all_to_all(out_weight, 'ch', split_axis=1, concat_axis=0, tiled=True)  189 us
    all_gather x1, waiting for transfers between devices, shards(): lax.all_gather(tokens, 'ch', axis=1, tiled=True)  112 us
    gather x2, local copies, waits for them, and re-layouts, shards(): jnp.take(kernel_rows, jnp.maximum(lag_grid, 0), axis=0)  99.7 us
    dot_general x1, matrix products, shards(): inner = jnp.einsum('ijc,njc->nic', toeplitz, blocks, precision=HIGH)  56 us
    dot_general x1, matrix products, shards(): jnp.einsum('tk,pkc->ptc', lax.all_gather(tokens, 'ch', axis=1, tiled=True...  18.3 us
    unnamed x45, local copies, waits for them, and re-layouts  16.4 us
    all_gather x2, blocking collectives, prefix(): lax.all_gather(a.astype(kind), axis)  13.2 us
  transfers between devices with their start and end apart: 3, of which 2 were waited for; matrix products, arithmetic and copies ran while one was open for 24% of the time, Pallas kernels for 0%

commit v1 on v0

v1 whole, which is shorter than its diff:
```python
import functools

import jax
import jax.numpy as jnp
from jax import lax
from jax.experimental import pallas as pl
from jax.experimental.pallas import tpu as pltpu
from jax.sharding import PartitionSpec as P

HALO = 16
TILE = 128


def features(part, start, size, proj_ref, filters_ref):
    window = proj_ref[part, pl.ds(start, size + HALO), :].astype(jnp.float32)
    total = None
    for lag in range(filters_ref.shape[1]):
        term = filters_ref[part, lag : lag + 1, :] * window[HALO - lag : HALO - lag + size]
        total = term if total is None else total + term
    return total


def state_kernel(seq, proj_ref, filters_ref, rates_ref, mixed_ref, state_ref):
    rows = mixed_ref.shape[0]
    decay = jnp.exp(rates_ref[...] * (-1.0 / seq))

    def tile(t, state):
        start = pl.multiple_of(t * TILE, TILE)
        keyed = features(1, start, TILE, proj_ref, filters_ref)
        valued = features(2, start, TILE, proj_ref, filters_ref)
        mixed_ref[pl.ds(start, TILE), :] = keyed * valued

        def group(g, state):
            base = pl.multiple_of(start + g * 8, 8)
            for i in range(8):
                state = decay * state + mixed_ref[pl.ds(base + i, 1), :]
            return state

        return lax.fori_loop(0, TILE // 8, group, state)

    state_ref[...] = lax.fori_loop(0, rows // TILE, tile, jnp.zeros_like(decay))


def conv_kernel(
    seq, proj_ref, mixed_ref, filters_ref, rates_ref, residues_ref, gain_ref, state_ref, out_ref, conv
):
    rows = mixed_ref.shape[0]
    decay = jnp.exp(rates_ref[...] * (-1.0 / seq))
    weight = residues_ref[...]
    gain = gain_ref[...]

    def tile(t, state):
        start = pl.multiple_of(t * TILE, TILE)

        def group(g, state):
            base = pl.multiple_of(start + g * 8, 8)
            parts = []
            for i in range(8):
                state = decay * state + mixed_ref[pl.ds(base + i, 1), :]
                parts.append(jnp.sum(weight * state, axis=0, keepdims=True))
            conv[pl.ds(pl.multiple_of(g * 8, 8), 8), :] = (
                jnp.concatenate(parts, 0) + gain * mixed_ref[pl.ds(base, 8), :]
            )
            return state

        state = lax.fori_loop(0, TILE // 8, group, state)
        query = features(0, start, TILE, proj_ref, filters_ref)
        out_ref[pl.ds(start, TILE), :] = (query * conv[...]).astype(out_ref.dtype)
        return state

    lax.fori_loop(0, rows // TILE, tile, state_ref[...])


def shards(tokens, in_weight, short_filters, log_rates, residues, skip_gain, out_weight):
    rows = tokens.shape[0]
    cols = in_weight.shape[2]
    ctx = lax.axis_size("ctx")
    seq = rows * ctx
    taps = short_filters.shape[1]
    modes = log_rates.shape[0]
    place = lax.axis_index("ctx")
    projected = jnp.einsum(
        "tk,pkc->ptc",
        lax.all_gather(tokens, "ch", axis=1, tiled=True),
        in_weight,
        preferred_element_type=jnp.float32,
    ).astype(jnp.bfloat16)
    previous = lax.ppermute(
        projected[:, rows - (taps - 1) :, :], "ctx", [(i, i + 1) for i in range(ctx - 1)]
    )
    extended = jnp.concatenate(
        [jnp.zeros((3, HALO - taps + 1, cols), jnp.bfloat16), previous, projected], axis=1
    )
    vmem = pl.BlockSpec(memory_space=pltpu.VMEM)
    params = pltpu.CompilerParams(vmem_limit_bytes=40 * 2**20)
    mixed, local = pl.pallas_call(
        functools.partial(state_kernel, seq),
        out_shape=(
            jax.ShapeDtypeStruct((rows, cols), jnp.float32),
            jax.ShapeDtypeStruct((modes, cols), jnp.float32),
        ),
        in_specs=[vmem] * 3,
        out_specs=(vmem, vmem),
        compiler_params=params,
    )(extended, short_filters, log_rates)
    gathered = lax.all_gather(local.astype(jnp.bfloat16), "ctx").astype(jnp.float32)
    hops = (place - 1 - jnp.arange(ctx))[:, None, None]
    spans = jnp.exp(-(log_rates / ctx)[None] * jnp.maximum(hops, 0).astype(jnp.float32))
    incoming = jnp.sum(jnp.where(hops >= 0, spans * gathered, 0.0), axis=0)
    gated = pl.pallas_call(
        functools.partial(conv_kernel, seq),
        out_shape=jax.ShapeDtypeStruct((rows, cols), jnp.bfloat16),
        in_specs=[vmem] * 7,
        out_specs=vmem,
        scratch_shapes=[pltpu.VMEM((TILE, cols), jnp.float32)],
        compiler_params=params,
    )(extended, mixed, short_filters, log_rates, residues, skip_gain[None, :], incoming)
    partial = jnp.dot(gated, out_weight, preferred_element_type=jnp.float32).astype(jnp.bfloat16)
    return lax.psum_scatter(partial, "ch", scatter_dimension=1, tiled=True)


def solution(mesh):
    return jax.shard_map(
        shards,
        mesh=mesh,
        in_specs=(
            P("ctx", "ch"),
            P(None, None, "ch"),
            P(None, None, "ch"),
            P(None, "ch"),
            P(None, "ch"),
            P("ch"),
            P("ch", None),
        ),
        out_specs=P("ctx", "ch"),
        check_vma=False,
    )
```

time: 603 us -> 354 us (0.59); the launches traced: 595 us -> 353 us
  blocking collectives: 202 us -> 7.55 us
  waiting for transfers between devices: 114 us -> 279 us
  local copies, waits for them, and re-layouts: 136 us -> 11.4 us
  matrix products: 101 us -> 25 us
  other arithmetic: 25.8 us -> 0.88 us
  Pallas kernels: 0 us -> 14.4 us
    all_to_all x1 -> x0, blocking collectives: 189 us -> none  [shards(): lax.all_to_all(out_weight, 'ch', split_axis=1, concat_axis=0, tiled=True)]
    reduce_scatter x0 -> x1, waiting for transfers between devices: none -> 148 us  [shards(): return lax.psum_scatter(partial, 'ch', scatter_dimension=1, tiled=True)]
    gather x2 -> x0, local copies, waits for them, and re-layouts: 99.7 us -> none  [shards(): jnp.take(kernel_rows, jnp.maximum(lag_grid, 0), axis=0)]
    dot_general x4 -> x1, matrix products: 82.4 us -> 6.78 us  [shards(): jnp.dot(gated, out_weight, preferred_element_type=jnp.float32)]
    all_gather x1, waiting for transfers between devices: 112 us -> 129 us  [shards(): lax.all_gather(tokens, 'ch', axis=1, tiled=True)]
    unnamed x45 -> x12, local copies, waits for them, and re-layouts: 16.4 us -> 0.03 us
    pallas_call x0 -> x2, Pallas kernels: none -> 14.4 us  [the longest x1 10 us: shards(): pl.pallas_call(functools.partial(conv_kernel, seq), out_shape=jax.ShapeDt...]
    concatenate x0 -> x1, local copies, waits for them, and re-layouts: none -> 11.3 us  [shards(): jnp.concatenate([jnp.zeros((3, HALO - taps + 1, cols), jnp.bfloat16), pre...]
  transfers between devices with their start and end apart: 3 -> 3, of which waited for: 2 -> 3; matrix products, arithmetic and copies ran while one was open for 24% -> 0% of each run, Pallas kernels for 0% -> 0%
where the time goes in v1:
time: 354 us; the launch traced here: 353 us
  waiting for transfers between devices  279 us (79%)
  matrix products  25 us (7%)
  Pallas kernels  14.4 us (4%)
  between operations  13.6 us (4%)
  local copies, waits for them, and re-layouts  11.4 us (3%)
  blocking collectives  7.55 us (2%)
    reduce_scatter x1, waiting for transfers between devices, shards(): return lax.psum_scatter(partial, 'ch', scatter_dimension=1, tiled=True)  148 us
    all_gather x1, waiting for transfers between devices, shards(): lax.all_gather(tokens, 'ch', axis=1, tiled=True)  129 us
    dot_general x1, matrix products, shards(): jnp.einsum('tk,pkc->ptc', lax.all_gather(tokens, 'ch', axis=1, tiled=True...  18.2 us
    concatenate x1, local copies, waits for them, and re-layouts, shards(): jnp.concatenate([jnp.zeros((3, HALO - taps + 1, cols), jnp.bfloat16), pre...  11.3 us
    pallas_call x1, Pallas kernels, shards(): pl.pallas_call(functools.partial(conv_kernel, seq), out_shape=jax.ShapeDt...  10 us
    all_gather x1, blocking collectives, shards(): lax.all_gather(local.astype(jnp.bfloat16), 'ctx').astype(jnp.float32)  7.55 us
  transfers between devices with their start and end apart: 3, of which 3 were waited for; matrix products, arithmetic and copies ran while one was open for 0% of the time, Pallas kernels for 0%

profile of v1, /device:TPU:0, one launch (start us, length us, event | category | flops | bytes accessed | tf_op | source)
XLA Modules:
  0.0 353.5 jit_solution(5834141477649803699)
XLA Ops:
  6.5 0.0 all-gather.3.cloned.1.call-start
  6.5 0.7 all-gather.3.cloned.1.call-update
  7.3 0.0 reduce-scatter.2.cloned.1.call-start
  7.3 0.8 multiply_negate_fusion
  8.1 129.4 %all-gather.3.cloned.1.call-done = bf16[1024,4096]{1,0:T(8,128)(2,1)} async-done(((bf16[1024,512]{1,0:T(8,128)(2,1)}), bf16[1024,4096]{1,0:T(8,128)(2,1)}) %all-gather.3.cloned.1.call-update) | async-done | bytes 8388624 | tf_op jit(solution)/shard_map/all_gather | solution.py:84
  137.5 18.2 %convert_bitcast_fusion = bf16[3,1024,512]{2,1,0:T(8,128)(2,1)S(1)} fusion(bf16[3,4096,512]{2,1,0:T(8,128)(2,1)} %param.8, bf16[1024,4096]{1,0:T(8,128)(2,1)} %all-gather.3.cloned.1.call-done), kind=kOutput, calls=%fused_computation.3 | convolution fusion | flops 12886474752 | bytes 24117248 | tf_op jit(solution)/shard_map/tk,pkc->ptc/dot_general | solution.py:82
  155.7 0.0 copy-start.4
  155.7 0.0 copy-start.2
  155.7 0.0 copy-start.3
  155.8 1.4 collective-permute-start
  157.2 0.8 collective-permute-done
  158.0 0.0 copy-done.4
  158.0 11.3 %concatenate.3.proj_ref = bf16[3,1040,512]{2,1,0:T(8,128)(2,1)S(1)} concatenate(bf16[3,14,512]{2,1,0:T(8,128)(2,1)S(1)} %broadcast_in_dim.20, bf16[3,2,512]{2,1,0:T(2,128)(2,1)S(1)} %collective-permute-done, bf16[3,1024,512]{2,1,0:T(8,128)(2,1)} %copy-done.4), dimensions={1} | concatenate | bytes 6389760 | tf_op jit(solution)/shard_map/concatenate | solution.py:91
  169.3 0.0 copy-done
  169.3 0.0 copy-done.1
  169.3 0.0 copy-start.5
  169.4 4.4 %shard_map.73 = (f32[1024,512]{1,0:T(8,128)S(1)}, f32[16,512]{1,0:T(8,128)S(1)}) custom-call(bf16[3,1040,512]{2,1,0:T(8,128)(2,1)S(1)} %concatenate.3.proj_ref, f32[3,3,512]{2,1,0:T(4,128)S(1)} %copy-done.1, f32[16,512]{1,0:T(8,128)S(1)} %copy-done), custom_call_target="tpu_custom_call" | custom-call | tf_op jit(solution)/shard_map/pallas_call | solution.py:96
  173.8 7.6 %all-gather = bf16[64,512]{1,0:T(8,128)(2,1)S(1)} all-gather(bf16[16,512]{1,0:T(8,128)(2,1)S(1)} %convert_element_type.26), channel_id=2, replica_groups=mesh['ctx'=4,'ch'=8] {'ctx'}, dimensions={0}, use_global_device_ids=true | all-gather | bytes 81920 | tf_op jit(solution)/shard_map/all_gather | solution.py:106
  181.3 0.1 fusion.5.state_ref
  181.4 0.0 copy-done.2
  181.4 10.0 %shard_map.74 = bf16[1024,512]{1,0:T(8,128)(2,1)S(1)} custom-call(bf16[3,1040,512]{2,1,0:T(8,128)(2,1)S(1)} %concatenate.3.proj_ref, f32[1024,512]{1,0:T(8,128)S(1)} %get-tuple-element.7.mixed_ref, f32[3,3,512]{2,1,0:T(4,128)S(1)} %copy-done.1, f32[16,512]{1,0:T(8,128)S(1)} %copy-done, f32[16,512]{1,0:T(8,128)S(1)} %copy-done.2, f32[1,512]{1,0:T(1,128)S(1)} %bitcast.13, ...), custom_call_target="tpu_custom_call" | custom-call | tf_op jit(solution)/shard_map/pallas_call | solution.py:110
  191.5 6.8 %convolution_convert_fusion = bf16[1024,4096]{1,0:T(8,128)(2,1)} fusion(bf16[1024,512]{1,0:T(8,128)(2,1)S(1)} %shard_map.74, bf16[512,4096]{1,0:T(8,128)(2,1)S(1)} %copy-done.5), kind=kOutput, calls=%fused_computation.2 | convolution fusion | flops 4299161600 | bytes 13631488 | tf_op jit(solution)/shard_map/dot_general | solution.py:118
  198.3 0.0 reduce-scatter.2.cloned.1.call-update
  198.3 148.3 %reduce-scatter.2.cloned.1.call-done = bf16[1024,512]{1,0:T(8,128)(2,1)} async-done(((bf16[1024,4096]{1,0:T(8,128)(2,1)}), bf16[1024,512]{1,0:T(8,128)(2,1)}) %reduce-scatter.2.cloned.1.call-update) | async-done | bytes 1048592 | tf_op jit(solution)/shard_map/reduce_scatter | solution.py:119
  (9 shorter events, 0.0 us)
Async XLA Ops:
  6.5 131.0 %all-gather.3.cloned.1.call-start = ((), (), s32[]{:S(2)}) async-start(), calls=%async_computation.1 | async-start | bytes 9437184 | tf_op jit(solution)/shard_map/all_gather | solution.py:84
  7.3 339.4 %reduce-scatter.2.cloned.1.call-start = ((), (), s32[]{:S(2)}) async-start(), calls=%async_computation.2 | async-start | bytes 9437184 | tf_op jit(solution)/shard_map/reduce_scatter | solution.py:119
  8.1 161.2 %copy-start = (f32[16,512]{1,0:T(8,128)S(1)}, f32[16,512]{1,0:T(8,128)}, u32[]{:S(2)}) copy-start(f32[16,512]{1,0:T(8,128)} %rates_ref.3) | copy-start | bytes 98308
  8.1 161.3 %copy-start.1 = (f32[3,3,512]{2,1,0:T(4,128)S(1)}, f32[3,3,512]{2,1,0:T(4,128)}, u32[]{:S(2)}) copy-start(f32[3,3,512]{2,1,0:T(4,128)} %filters_ref.3) | copy-start | bytes 55300
  155.7 2.3 copy-start.4
  155.7 25.7 %copy-start.2 = (f32[16,512]{1,0:T(8,128)S(1)}, f32[16,512]{1,0:T(8,128)}, u32[]{:S(2)}) copy-start(f32[16,512]{1,0:T(8,128)} %residues_ref.1) | copy-start | bytes 98308
  155.7 25.7 %copy-start.3 = (f32[512]{0:T(512)S(1)}, f32[512]{0:T(512)}, u32[]{:S(2)}) copy-start(f32[512]{0:T(512)} %param.12) | copy-start | bytes 6148
  155.8 2.2 collective-permute-start
  169.3 22.1 %copy-start.5 = (bf16[512,4096]{1,0:T(8,128)(2,1)S(1)}, bf16[512,4096]{1,0:T(8,128)(2,1)}, u32[]{:S(2)}) copy-start(bf16[512,4096]{1,0:T(8,128)(2,1)} %param.13) | copy-start | bytes 12582916
Sparse Core Ops, SparseCore 0:
  9.4 128.0 all-gather.2
  198.4 148.1 reduce-scatter.1

commit v2 on v1

v2 whole, which is shorter than its diff:
```python
import functools

import jax
import jax.numpy as jnp
from jax import lax
from jax.experimental import pallas as pl
from jax.experimental.pallas import tpu as pltpu
from jax.sharding import PartitionSpec as P

HALO = 16
TILE = 128
PIECE = 256


def features(part, start, size, proj_ref, filters_ref):
    window = proj_ref[part, pl.ds(start, size + HALO), :].astype(jnp.float32)
    total = None
    for lag in range(filters_ref.shape[1]):
        term = filters_ref[part, lag : lag + 1, :] * window[HALO - lag : HALO - lag + size]
        total = term if total is None else total + term
    return total


def remote(source, target, send, receive, device):
    return pltpu.make_async_remote_copy(
        src_ref=source,
        dst_ref=target,
        send_sem=send,
        recv_sem=receive,
        device_id=device,
        device_id_type=pl.DeviceIdType.MESH,
    )


def greet(outer, inner, place, count, ctx):
    barrier = pltpu.get_barrier_semaphore()

    def signal(device):
        pl.semaphore_signal(
            barrier, inc=1, device_id=device, device_id_type=pl.DeviceIdType.MESH
        )

    signal({"ch": outer * 2 + 1 - inner})

    @pl.when(outer > 0)
    def _():
        signal({"ch": (outer - 1) * 2 + inner})

    @pl.when(outer < count - 1)
    def _():
        signal({"ch": (outer + 1) * 2 + inner})

    for hop in range(1, ctx):
        signal({"ctx": lax.rem(place + hop, ctx)})
    near = (outer + count - 1) // count + (2 * count - 2 - outer) // count
    pl.semaphore_wait(barrier, ctx + near)


def project_kernel(
    count, ctx, tokens_ref, weight_ref, filters_ref, rates_ref,
    ext_ref, mixed_ref, incoming_ref,
    gath, weight, acc, halo, local, states,
    local_sem, send_z, send_x, recv, halo_sem, state_send, state_recv,
):
    place = lax.axis_index("ctx")
    me = lax.axis_index("ch")
    outer, inner = me // 2, lax.rem(me, 2)
    rows, depth = tokens_ref.shape
    seq = rows * ctx
    pieces = rows // PIECE
    own = pltpu.make_async_copy(tokens_ref, gath.at[me], local_sem.at[0])
    own.start()
    loads = [
        pltpu.make_async_copy(weight_ref.at[p], weight.at[p], local_sem.at[1 + p]) for p in range(3)
    ]
    for load in loads:
        load.start()
    greet(outer, inner, place, count, ctx)
    own.wait()

    def span(r):
        return pl.ds(pl.multiple_of(r * PIECE, PIECE), PIECE)

    def along(source, r, up):
        slot = source * 2 + inner
        block = gath.at[slot, span(r)]
        step = 1 if up else -1
        return remote(
            block, block, send_z.at[0 if up else 1, source, r], recv.at[slot, r],
            {"ch": (outer + step) * 2 + inner},
        )

    def across(source, r):
        slot = source * 2 + inner
        block = gath.at[slot, span(r)]
        return remote(
            block, block, send_x.at[source, r], recv.at[slot, r],
            {"ch": outer * 2 + 1 - inner},
        )

    def arrived(slot, r):
        block = gath.at[slot, span(r)]
        remote(block, block, send_x.at[0, 0], recv.at[slot, r], {"ch": outer * 2 + 1 - inner}).wait_recv()

    def multiply(slot, r, first=False):
        block = gath[slot, span(r), :]
        for p in range(3):
            term = jnp.dot(
                block,
                weight[p, pl.ds(pl.multiple_of(slot * depth, depth), depth), :],
                preferred_element_type=jnp.float32,
            )
            if first:
                acc[p, span(r), :] = term
            else:
                acc[p, span(r), :] += term

    def begin(r, carry):
        across(outer, r).start()

        @pl.when(outer < count - 1)
        def _():
            along(outer, r, True).start()

        @pl.when(outer > 0)
        def _():
            along(outer, r, False).start()

        return carry

    lax.fori_loop(0, pieces, begin, 0)
    for load in loads:
        load.wait()

    def start(r, carry):
        multiply(me, r, True)
        return carry

    lax.fori_loop(0, pieces, start, 0)

    def take(slot, r):
        arrived(slot, r)
        multiply(slot, r)

    def beside(distance):
        other = 1 - inner

        def one(r, carry):
            if distance == 0:
                take(outer * 2 + other, r)
                return carry

            @pl.when(outer >= distance)
            def _():
                take((outer - distance) * 2 + other, r)

            @pl.when(outer + distance < count)
            def _():
                take((outer + distance) * 2 + other, r)

            return carry

        lax.fori_loop(0, pieces, one, 0)

    for distance in range(1, count):

        def one(r, carry, distance=distance):
            @pl.when(outer >= distance)
            def _():
                source = outer - distance
                arrived(source * 2 + inner, r)

                @pl.when(outer < count - 1)
                def _():
                    along(source, r, True).start()

                across(source, r).start()
                multiply(source * 2 + inner, r)

            @pl.when(outer + distance < count)
            def _():
                source = outer + distance
                arrived(source * 2 + inner, r)

                @pl.when(outer > 0)
                def _():
                    along(source, r, False).start()

                across(source, r).start()
                multiply(source * 2 + inner, r)

            return carry

        lax.fori_loop(0, pieces, one, 0)
        beside(distance - 1)
    beside(count - 1)

    def settle(t, carry):
        base = pl.multiple_of(rows - (t + 1) * TILE, TILE)
        for p in range(3):
            ext_ref[p, pl.ds(HALO + base, TILE), :] = acc[p, pl.ds(base, TILE), :].astype(ext_ref.dtype)
        return carry

    settle(0, 0)
    edge = remote(
        ext_ref.at[:, pl.ds(rows, HALO), :], halo, halo_sem.at[0], halo_sem.at[1],
        {"ctx": lax.rem(place + 1, ctx)},
    )

    @pl.when(place < ctx - 1)
    def _():
        edge.start()

    lax.fori_loop(1, rows // TILE, settle, 0)

    @pl.when(place > 0)
    def _():
        edge.wait_recv()
        ext_ref[:, :HALO, :] = halo[...]

    @pl.when(place == 0)
    def _():
        ext_ref[:, :HALO, :] = jnp.zeros_like(halo)

    rate = rates_ref[...]
    decay = jnp.exp(rate * (-1.0 / seq))

    def tile(t, state):
        base = pl.multiple_of(t * TILE, TILE)
        keyed = features(1, base, TILE, ext_ref, filters_ref)
        valued = features(2, base, TILE, ext_ref, filters_ref)
        mixed_ref[pl.ds(base, TILE), :] = keyed * valued

        def group(g, state):
            row = pl.multiple_of(base + g * 8, 8)
            for i in range(8):
                state = decay * state + mixed_ref[pl.ds(row + i, 1), :]
            return state

        return lax.fori_loop(0, TILE // 8, group, state)

    local[...] = lax.fori_loop(0, rows // TILE, tile, jnp.zeros_like(decay))
    sends = [
        remote(
            local, states.at[hop - 1], state_send.at[hop - 1], state_recv.at[hop - 1],
            {"ctx": lax.rem(place + hop, ctx)},
        )
        for hop in range(1, ctx)
    ]
    for send in sends:
        send.start()
    total = jnp.zeros_like(decay)
    for hop in range(1, ctx):
        sends[hop - 1].wait_recv()
        term = jnp.exp(rate * (-(hop - 1) / ctx)) * states[hop - 1]
        total = total + jnp.where(place >= hop, term, 0.0)
    incoming_ref[...] = total
    for send in sends:
        send.wait_send()

    @pl.when(place < ctx - 1)
    def _():
        edge.wait_send()

    def drain(r, carry):
        for source in range(count):
            across(source, r).wait_send()

            @pl.when(jnp.logical_and(outer >= source, outer < count - 1))
            def _():
                along(source, r, True).wait_send()

            @pl.when(jnp.logical_and(outer <= source, outer > 0))
            def _():
                along(source, r, False).wait_send()

        return carry

    lax.fori_loop(0, pieces, drain, 0)


def output_kernel(
    count, ctx, ext_ref, mixed_ref, filters_ref, rates_ref, residues_ref, gain_ref, state_ref,
    weight_ref, out_ref,
    conv, gated, stage, beside, chain, send_x, recv_x, send_z, recv_z,
):
    me = lax.axis_index("ch")
    outer, inner = me // 2, lax.rem(me, 2)
    rows, width = out_ref.shape
    seq = rows * ctx
    pieces = rows // PIECE
    greet(outer, inner, 0, count, 1)
    decay = jnp.exp(rates_ref[...] * (-1.0 / seq))
    residue = residues_ref[...]
    gain = gain_ref[...]
    far = (count - 1) * (1 - outer // (count // 2))

    def span(r):
        return pl.ds(pl.multiple_of(r * PIECE, PIECE), PIECE)

    def partial(block, r):
        return jnp.dot(
            gated[span(r), :],
            weight_ref[:, pl.ds(pl.multiple_of(block * width, width), width)],
            preferred_element_type=jnp.float32,
        )

    def across(target, r):
        return remote(
            stage.at[target, span(r)], beside.at[target, span(r)],
            send_x.at[target, r], recv_x.at[target, r],
            {"ch": outer * 2 + 1 - inner},
        )

    def along(target, r, up, last):
        slot = count if last and not up else target
        step = 1 if up else -1
        return remote(
            beside.at[target, span(r)], chain.at[slot, span(r)],
            send_z.at[target, r], recv_z.at[slot, r],
            {"ch": (outer + step) * 2 + inner},
        )

    def received(slot, r):
        block = chain.at[slot, span(r)]
        remote(
            block, block, send_z.at[0, 0], recv_z.at[slot, r], {"ch": outer * 2 + 1 - inner}
        ).wait_recv()
        return chain[slot, span(r), :].astype(jnp.float32)

    def give(target, r):
        stage[target, span(r), :] = partial(target * 2 + 1 - inner, r).astype(stage.dtype)
        across(target, r).start()

    def first(r, state):
        base = pl.multiple_of(r * PIECE, PIECE)

        def group(g, state):
            row = pl.multiple_of(base + g * 8, 8)
            parts = []
            for i in range(8):
                state = decay * state + mixed_ref[pl.ds(row + i, 1), :]
                parts.append(jnp.sum(residue * state, axis=0, keepdims=True))
            conv[pl.ds(pl.multiple_of(g * 8, 8), 8), :] = (
                jnp.concatenate(parts, 0) + gain * mixed_ref[pl.ds(row, 8), :]
            )
            return state

        state = lax.fori_loop(0, PIECE // 8, group, state)
        query = features(0, base, PIECE, ext_ref, filters_ref)
        gated[span(r), :] = (query * conv[...]).astype(gated.dtype)
        give(far, r)
        return state

    lax.fori_loop(0, pieces, first, state_ref[...])
    for distance in range(count - 2, -1, -1):

        def rest(r, carry, distance=distance):
            @pl.when(jnp.logical_and(outer + distance < count, outer + distance != far))
            def _():
                give(outer + distance, r)

            if distance:

                @pl.when(jnp.logical_and(outer >= distance, outer - distance != far))
                def _():
                    give(outer - distance, r)

            return carry

        lax.fori_loop(0, pieces, rest, 0)

    def total(target, r):
        mine = partial(target * 2 + inner, r)
        across(target, r).wait_recv()
        return mine + beside[target, span(r), :].astype(jnp.float32)

    for distance in range(count - 1, 0, -1):

        def hop(r, carry, distance=distance):
            @pl.when(outer + distance < count)
            def _():
                target = outer + distance
                conv[...] = total(target, r)

                @pl.when(outer > 0)
                def _():
                    conv[...] += received(target, r)

                beside[target, span(r), :] = conv[...].astype(beside.dtype)
                along(target, r, True, distance == 1).start()

            @pl.when(outer >= distance)
            def _():
                target = outer - distance
                conv[...] = total(target, r)

                @pl.when(outer < count - 1)
                def _():
                    conv[...] += received(target, r)

                beside[target, span(r), :] = conv[...].astype(beside.dtype)
                along(target, r, False, distance == 1).start()

            return carry

        lax.fori_loop(0, pieces, hop, 0)

    def finish(r, carry):
        conv[...] = total(outer, r)

        @pl.when(outer > 0)
        def _():
            conv[...] += received(outer, r)

        @pl.when(outer < count - 1)
        def _():
            conv[...] += received(count, r)

        out_ref[span(r), :] = conv[...].astype(out_ref.dtype)
        return carry

    lax.fori_loop(0, pieces, finish, 0)

    def drain(r, carry):
        for target in range(count):
            across(target, r).wait_send()

            @pl.when(outer != target)
            def _():
                along(target, r, True, False).wait_send()

        return carry

    lax.fori_loop(0, pieces, drain, 0)


def shards(tokens, in_weight, short_filters, log_rates, residues, skip_gain, out_weight):
    rows, depth = tokens.shape
    cols = in_weight.shape[2]
    ctx = lax.axis_size("ctx")
    ways = lax.axis_size("ch")
    count = ways // 2
    modes = log_rates.shape[0]
    pieces = rows // PIECE
    vmem = pl.BlockSpec(memory_space=pltpu.VMEM)
    anywhere = pl.BlockSpec(memory_space=pl.ANY)
    dma = pltpu.SemaphoreType.DMA
    f32, bf16 = jnp.float32, jnp.bfloat16
    extended, mixed, incoming = pl.pallas_call(
        functools.partial(project_kernel, count, ctx),
        out_shape=(
            jax.ShapeDtypeStruct((3, HALO + rows, cols), bf16),
            jax.ShapeDtypeStruct((rows, cols), f32),
            jax.ShapeDtypeStruct((modes, cols), f32),
        ),
        in_specs=[anywhere, anywhere, vmem, vmem],
        out_specs=(vmem, vmem, vmem),
        scratch_shapes=[
            pltpu.VMEM((ways, rows, depth), bf16),
            pltpu.VMEM((3, ways * depth, cols), bf16),
            pltpu.VMEM((3, rows, cols), f32),
            pltpu.VMEM((3, HALO, cols), bf16),
            pltpu.VMEM((modes, cols), f32),
            pltpu.VMEM((ctx - 1, modes, cols), f32),
            dma((4,)),
            dma((2, count, pieces)),
            dma((count, pieces)),
            dma((ways, pieces)),
            dma((2,)),
            dma((ctx - 1,)),
            dma((ctx - 1,)),
        ],
        compiler_params=pltpu.CompilerParams(
            collective_id=0, has_side_effects=True, vmem_limit_bytes=48 * 2**20
        ),
    )(tokens, in_weight, short_filters, log_rates)
    return pl.pallas_call(
        functools.partial(output_kernel, count, ctx),
        out_shape=jax.ShapeDtypeStruct((rows, depth), bf16),
        in_specs=[vmem] * 8,
        out_specs=vmem,
        scratch_shapes=[
            pltpu.VMEM((PIECE, cols), f32),
            pltpu.VMEM((rows, cols), bf16),
            pltpu.VMEM((count, rows, depth), bf16),
            pltpu.VMEM((count, rows, depth), bf16),
            pltpu.VMEM((count + 1, rows, depth), bf16),
            dma((count, pieces)),
            dma((count, pieces)),
            dma((count, pieces)),
            dma((count + 1, pieces)),
        ],
        compiler_params=pltpu.CompilerParams(
            collective_id=1, has_side_effects=True, vmem_limit_bytes=48 * 2**20
        ),
    )(
        extended, mixed, short_filters, log_rates, residues, skip_gain[None, :], incoming, out_weight
    )


def solution(mesh):
    return jax.shard_map(
        shards,
        mesh=mesh,
        in_specs=(
            P("ctx", "ch"),
            P(None, None, "ch"),
            P(None, None, "ch"),
            P(None, "ch"),
            P(None, "ch"),
            P("ch"),
            P("ch", None),
        ),
        out_specs=P("ctx", "ch"),
        check_vma=False,
    )
```

time: 354 us -> 212 us (0.60)
  waiting for transfers between devices: 279 us -> 0 us
  Pallas kernels: 14.4 us -> 208 us
  matrix products: 25 us -> 0 us
  between operations: 13.6 us -> 0.05 us
  local copies, waits for them, and re-layouts: 11.4 us -> 3.7 us
  blocking collectives: 7.55 us -> 0 us
    pallas_call x2, Pallas kernels: 14.4 us -> 208 us  [the longest x1 108 us: shards(): pl.pallas_call(functools.partial(project_kernel, count, ctx), out_shape=(...]
    reduce_scatter x1 -> x0, waiting for transfers between devices: 148 us -> none  [shards(): return lax.psum_scatter(partial, 'ch', scatter_dimension=1, tiled=True)]
    all_gather x1 -> x0, waiting for transfers between devices: 129 us -> none  [shards(): lax.all_gather(tokens, 'ch', axis=1, tiled=True)]
    dot_general x2 -> x0, matrix products: 25 us -> none  [the longest x1 18.2 us: shards(): jnp.einsum('tk,pkc->ptc', lax.all_gather(tokens, 'ch', axis=1, tiled=True...]
    concatenate x1 -> x0, local copies, waits for them, and re-layouts: 11.3 us -> none  [shards(): jnp.concatenate([jnp.zeros((3, HALO - taps + 1, cols), jnp.bfloat16), pre...]
    all_gather x1 -> x0, blocking collectives: 7.55 us -> none  [shards(): lax.all_gather(local.astype(jnp.bfloat16), 'ctx').astype(jnp.float32)]
    unnamed x12 -> x13, local copies, waits for them, and re-layouts: 0.03 us -> 3.7 us
  transfers between devices with their start and end apart: 3 -> 0, of which waited for: 3 -> 0; matrix products, arithmetic and copies ran while one was open for 0% -> 0% of each run, Pallas kernels for 0% -> 0%
where the time goes in v2:
time: 212 us
  Pallas kernels  208 us (98%)
  local copies, waits for them, and re-layouts  3.7 us (2%)
    pallas_call x1, Pallas kernels, shards(): pl.pallas_call(functools.partial(project_kernel, count, ctx), out_shape=(...  108 us
    pallas_call x1, Pallas kernels, shards(): pl.pallas_call(functools.partial(output_kernel, count, ctx), out_shape=ja...  99.7 us

profile of v2, /device:TPU:0, one launch (start us, length us, event | category | flops | bytes accessed | tf_op | source)
XLA Modules:
  0.0 211.5 jit_solution(12369932612339779249)
XLA Ops:
  0.0 0.0 copy-start
  0.0 1.2 copy-done
  1.2 0.0 copy-start.1
  1.2 0.8 copy-done.1
  2.0 0.0 copy-start.3
  2.0 0.7 copy-done.3
  2.7 0.0 copy-start.2
  2.7 0.0 copy-start.4
  2.7 0.0 copy-start.5
  2.7 108.1 %shard_map.73 = (bf16[3,1040,512]{2,1,0:T(8,128)(2,1)}, f32[1024,512]{1,0:T(8,128)S(1)}, f32[16,512]{1,0:T(8,128)S(1)}) custom-call(bf16[1024,512]{1,0:T(8,128)(2,1)S(1)} %copy-done, bf16[3,4096,512]{2,1,0:T(8,128)(2,1)} %weight_ref.2, f32[3,3,512]{2,1,0:T(4,128)S(1)} %copy-done.3, f32[16,512]{1,0:T(8,128)S(1)} %copy-done.1), custom_call_target="tpu_custom_call" | custom-call | tf_op jit(solution)/shard_map/pallas_call | solution.py:450
  110.8 0.0 copy-done.2
  110.8 0.0 copy-done.4
  110.8 0.0 copy-done.5
  110.9 99.7 %shard_map.74 = bf16[1024,512]{1,0:T(8,128)(2,1)S(1)} custom-call(bf16[3,1040,512]{2,1,0:T(8,128)(2,1)} %get-tuple-element.8.ext_ref, f32[1024,512]{1,0:T(8,128)S(1)} %get-tuple-element.9.mixed_ref, f32[3,3,512]{2,1,0:T(4,128)S(1)} %copy-done.3, f32[16,512]{1,0:T(8,128)S(1)} %copy-done.2, f32[16,512]{1,0:T(8,128)S(1)} %copy-done.4, f32[1,512]{1,0:T(1,128)S(1)} %bitcast.1, ...), custom_call_target="tpu_custom_call" | custom-call | tf_op jit(solution)/shard_map/pallas_call | solution.py:478
  210.6 1.0 copy.9
Async XLA Ops:
  0.0 1.2 copy-start
  1.2 0.8 copy-start.1
  2.0 0.7 copy-start.3
  2.7 108.1 %copy-start.2 = (f32[16,512]{1,0:T(8,128)S(1)}, f32[16,512]{1,0:T(8,128)}, u32[]{:S(2)}) copy-start(f32[16,512]{1,0:T(8,128)} %rates_ref.3) | copy-start | bytes 98308
  2.7 108.1 %copy-start.4 = (f32[16,512]{1,0:T(8,128)S(1)}, f32[16,512]{1,0:T(8,128)}, u32[]{:S(2)}) copy-start(f32[16,512]{1,0:T(8,128)} %residues_ref.1) | copy-start | bytes 98308
  2.7 108.1 %copy-start.5 = (f32[512]{0:T(512)S(1)}, f32[512]{0:T(512)}, u32[]{:S(2)}) copy-start(f32[512]{0:T(512)} %param.12) | copy-start | bytes 6148

commit v3 on v2

--- a/solution.py
+++ b/solution.py
@@ -60,7 +60,7 @@
     count, ctx, tokens_ref, weight_ref, filters_ref, rates_ref,
     ext_ref, mixed_ref, incoming_ref,
     gath, weight, acc, halo, local, states,
-    local_sem, send_z, send_x, recv, halo_sem, state_send, state_recv,
+    local_sem, send_z, send_x, recv, halo_sem, state_send, state_recv, send_pair,
 ):
     place = lax.axis_index("ctx")
     me = lax.axis_index("ch")
@@ -68,6 +68,8 @@
     rows, depth = tokens_ref.shape
     seq = rows * ctx
     pieces = rows // PIECE
+    half = pieces // 2
+    pair = outer + 1 - 2 * lax.rem(outer, 2)
     own = pltpu.make_async_copy(tokens_ref, gath.at[me], local_sem.at[0])
     own.start()
     loads = [
@@ -96,6 +98,18 @@
         return remote(
             block, block, send_x.at[source, r], recv.at[slot, r],
             {"ch": outer * 2 + 1 - inner},
+        )
+
+    def cross(source, r):
+        @pl.when(jnp.logical_or(source != pair, r >= half))
+        def _():
+            across(source, r).start()
+
+    def relay(r):
+        block = gath.at[outer * 2 + 1 - inner, span(r)]
+        return remote(
+            block, block, send_pair.at[r], recv.at[outer * 2 + 1 - inner, r],
+            {"ch": pair * 2 + inner},
         )
 
     def arrived(slot, r):
@@ -142,6 +156,9 @@
         arrived(slot, r)
         multiply(slot, r)
 
+    def direct(source, r):
+        return jnp.logical_or(source != pair, r >= half)
+
     def beside(distance):
         other = 1 - inner
 
@@ -150,11 +167,11 @@
                 take(outer * 2 + other, r)
                 return carry
 
-            @pl.when(outer >= distance)
+            @pl.when(jnp.logical_and(outer >= distance, direct(outer - distance, r)))
             def _():
                 take((outer - distance) * 2 + other, r)
 
-            @pl.when(outer + distance < count)
+            @pl.when(jnp.logical_and(outer + distance < count, direct(outer + distance, r)))
             def _():
                 take((outer + distance) * 2 + other, r)
 
@@ -174,7 +191,7 @@
                 def _():
                     along(source, r, True).start()
 
-                across(source, r).start()
+                cross(source, r)
                 multiply(source * 2 + inner, r)
 
             @pl.when(outer + distance < count)
@@ -186,14 +203,23 @@
                 def _():
                     along(source, r, False).start()
 
-                across(source, r).start()
+                cross(source, r)
                 multiply(source * 2 + inner, r)
 
             return carry
 
         lax.fori_loop(0, pieces, one, 0)
+        if distance == count - 1:
+            for r in range(half):
+                relay(r).start()
         beside(distance - 1)
     beside(count - 1)
+
+    def last(r, carry):
+        take(pair * 2 + 1 - inner, r)
+        return carry
+
+    lax.fori_loop(0, half, last, 0)
 
     def settle(t, carry):
         base = pl.multiple_of(rows - (t + 1) * TILE, TILE)
@@ -264,7 +290,10 @@
 
     def drain(r, carry):
         for source in range(count):
-            across(source, r).wait_send()
+
+            @pl.when(direct(source, r))
+            def _():
+                across(source, r).wait_send()
 
             @pl.when(jnp.logical_and(outer >= source, outer < count - 1))
             def _():
@@ -277,18 +306,22 @@
         return carry
 
     lax.fori_loop(0, pieces, drain, 0)
+    for r in range(half):
+        relay(r).wait_send()
 
 
 def output_kernel(
     count, ctx, ext_ref, mixed_ref, filters_ref, rates_ref, residues_ref, gain_ref, state_ref,
     weight_ref, out_ref,
-    conv, gated, stage, beside, chain, send_x, recv_x, send_z, recv_z,
+    conv, gated, stage, beside, chain, send_x, recv_x, send_z, recv_z, passed, recv_pair,
 ):
     me = lax.axis_index("ch")
     outer, inner = me // 2, lax.rem(me, 2)
     rows, width = out_ref.shape
     seq = rows * ctx
     pieces = rows // PIECE
+    half = pieces // 2
+    pair = outer + 1 - 2 * lax.rem(outer, 2)
     greet(outer, inner, 0, count, 1)
     decay = jnp.exp(rates_ref[...] * (-1.0 / seq))
     residue = residues_ref[...]
@@ -321,6 +354,12 @@
             {"ch": (outer + step) * 2 + inner},
         )
 
+    def relay(r):
+        return remote(
+            stage.at[pair, span(r)], passed.at[span(r)], send_x.at[pair, r], recv_pair.at[r],
+            {"ch": pair * 2 + inner},
+        )
+
     def received(slot, r):
         block = chain.at[slot, span(r)]
         remote(
@@ -330,7 +369,22 @@
 
     def give(target, r):
         stage[target, span(r), :] = partial(target * 2 + 1 - inner, r).astype(stage.dtype)
-        across(target, r).start()
+
+        @pl.when(jnp.logical_or(target != pair, r >= half))
+        def _():
+            across(target, r).start()
+
+        @pl.when(jnp.logical_and(target == pair, r < half))
+        def _():
+            relay(r).start()
+
+    def give_joined(r, carry):
+        relay(r).wait_recv()
+        stage[outer, span(r), :] = (
+            partial(outer * 2 + 1 - inner, r) + passed[span(r), :].astype(jnp.float32)
+        ).astype(stage.dtype)
+        across(outer, r).start()
+        return carry
 
     def first(r, state):
         base = pl.multiple_of(r * PIECE, PIECE)
@@ -356,12 +410,18 @@
     for distance in range(count - 2, -1, -1):
 
         def rest(r, carry, distance=distance):
-            @pl.when(jnp.logical_and(outer + distance < count, outer + distance != far))
-            def _():
-                give(outer + distance, r)
+            if distance == 0:
+
+                @pl.when(r >= half)
+                def _():
+                    give(outer, r)
 
             if distance:
 
+                @pl.when(jnp.logical_and(outer + distance < count, outer + distance != far))
+                def _():
+                    give(outer + distance, r)
+
                 @pl.when(jnp.logical_and(outer >= distance, outer - distance != far))
                 def _():
                     give(outer - distance, r)
@@ -371,9 +431,12 @@
         lax.fori_loop(0, pieces, rest, 0)
 
     def total(target, r):
-        mine = partial(target * 2 + inner, r)
-        across(target, r).wait_recv()
-        return mine + beside[target, span(r), :].astype(jnp.float32)
+        conv[...] = partial(target * 2 + inner, r)
+
+        @pl.when(jnp.logical_or(target != pair, r >= half))
+        def _():
+            across(target, r).wait_recv()
+            conv[...] += beside[target, span(r), :].astype(jnp.float32)
 
     for distance in range(count - 1, 0, -1):
 
@@ -381,7 +444,7 @@
             @pl.when(outer + distance < count)
             def _():
                 target = outer + distance
-                conv[...] = total(target, r)
+                total(target, r)
 
                 @pl.when(outer > 0)
                 def _():
@@ -393,7 +456,7 @@
             @pl.when(outer >= distance)
             def _():
                 target = outer - distance
-                conv[...] = total(target, r)
+                total(target, r)
 
                 @pl.when(outer < count - 1)
                 def _():
@@ -405,9 +468,11 @@
             return carry
 
         lax.fori_loop(0, pieces, hop, 0)
+        if distance == max(count - 2, 1):
+            lax.fori_loop(0, half, give_joined, 0)
 
     def finish(r, carry):
-        conv[...] = total(outer, r)
+        total(outer, r)
 
         @pl.when(outer > 0)
         def _():
@@ -470,6 +535,7 @@
             dma((2,)),
             dma((ctx - 1,)),
             dma((ctx - 1,)),
+            dma((max(1, pieces // 2),)),
         ],
         compiler_params=pltpu.CompilerParams(
             collective_id=0, has_side_effects=True, vmem_limit_bytes=48 * 2**20
@@ -490,6 +556,8 @@
             dma((count, pieces)),
             dma((count, pieces)),
             dma((count + 1, pieces)),
+            pltpu.VMEM((rows, depth), bf16),
+            dma((pieces,)),
         ],
         compiler_params=pltpu.CompilerParams(
             collective_id=1, has_side_effects=True, vmem_limit_bytes=48 * 2**20

time: 212 us -> 199 us (0.939)
  Pallas kernels: 208 us -> 195 us
    pallas_call x1, Pallas kernels: 108 us -> 98 us  [shards(): pl.pallas_call(functools.partial(project_kernel, count, ctx), out_shape=(...]
    pallas_call x1, Pallas kernels: 99.7 us -> 96.9 us  [shards(): pl.pallas_call(functools.partial(output_kernel, count, ctx), out_shape=ja...]
where the time goes in v3:
time: 199 us
  Pallas kernels  195 us (98%)
  local copies, waits for them, and re-layouts  3.7 us (2%)
    pallas_call x1, Pallas kernels, shards(): pl.pallas_call(functools.partial(project_kernel, count, ctx), out_shape=(...  98 us
    pallas_call x1, Pallas kernels, shards(): pl.pallas_call(functools.partial(output_kernel, count, ctx), out_shape=ja...  96.9 us

profile of v3, /device:TPU:0, one launch (start us, length us, event | category | flops | bytes accessed | tf_op | source)
XLA Modules:
  0.0 198.7 jit_solution(11172583413330330592)
XLA Ops:
  0.0 0.0 copy-start
  0.0 1.2 copy-done
  1.2 0.0 copy-start.1
  1.2 0.8 copy-done.1
  2.0 0.0 copy-start.3
  2.0 0.7 copy-done.3
  2.7 0.0 copy-start.2
  2.7 0.0 copy-start.4
  2.7 0.0 copy-start.5
  2.7 98.0 %shard_map.73 = (bf16[3,1040,512]{2,1,0:T(8,128)(2,1)}, f32[1024,512]{1,0:T(8,128)S(1)}, f32[16,512]{1,0:T(8,128)S(1)}) custom-call(bf16[1024,512]{1,0:T(8,128)(2,1)S(1)} %copy-done, bf16[3,4096,512]{2,1,0:T(8,128)(2,1)} %weight_ref.2, f32[3,3,512]{2,1,0:T(4,128)S(1)} %copy-done.3, f32[16,512]{1,0:T(8,128)S(1)} %copy-done.1), custom_call_target="tpu_custom_call" | custom-call | tf_op jit(solution)/shard_map/pallas_call | solution.py:515
  100.8 0.0 copy-done.2
  100.8 0.0 copy-done.4
  100.8 0.0 copy-done.5
  100.8 96.9 %shard_map.74 = bf16[1024,512]{1,0:T(8,128)(2,1)S(1)} custom-call(bf16[3,1040,512]{2,1,0:T(8,128)(2,1)} %get-tuple-element.8.ext_ref, f32[1024,512]{1,0:T(8,128)S(1)} %get-tuple-element.9.mixed_ref, f32[3,3,512]{2,1,0:T(4,128)S(1)} %copy-done.3, f32[16,512]{1,0:T(8,128)S(1)} %copy-done.2, f32[16,512]{1,0:T(8,128)S(1)} %copy-done.4, f32[1,512]{1,0:T(1,128)S(1)} %bitcast.1, ...), custom_call_target="tpu_custom_call" | custom-call | tf_op jit(solution)/shard_map/pallas_call | solution.py:544
  197.7 1.0 copy.9
Async XLA Ops:
  0.0 1.2 copy-start
  1.2 0.8 copy-start.1
  2.0 0.7 copy-start.3
  2.7 98.0 %copy-start.2 = (f32[16,512]{1,0:T(8,128)S(1)}, f32[16,512]{1,0:T(8,128)}, u32[]{:S(2)}) copy-start(f32[16,512]{1,0:T(8,128)} %rates_ref.3) | copy-start | bytes 98308
  2.7 98.1 %copy-start.4 = (f32[16,512]{1,0:T(8,128)S(1)}, f32[16,512]{1,0:T(8,128)}, u32[]{:S(2)}) copy-start(f32[16,512]{1,0:T(8,128)} %residues_ref.1) | copy-start | bytes 98308
  2.7 98.1 %copy-start.5 = (f32[512]{0:T(512)S(1)}, f32[512]{0:T(512)}, u32[]{:S(2)}) copy-start(f32[512]{0:T(512)} %param.12) | copy-start | bytes 6148
